TPU v7x, 32 devices: a whole 2x2x4 slice. The times are simulated.
32 devices in a mesh: dp: 8 (over z, y), ctx: 4 (over x, core).
Axes of the slice: x: 2, y: 2, z: 4, core: 2. Of those that a mesh axis runs over, the one named last changes fastest.
Arguments:
- projected: bfloat16 [2, 8, 512, 4096], P(None, 'dp', 'ctx'), may hold values from -6 to 6
- token_ids: int32 [8, 512], P('dp', 'ctx'), may hold values from 0 to 511
- short_filters: float32 [2, 7, 4096], P(None, None, 'ctx'), may hold values from -2 to 2
- medium_filter: bfloat16 [128, 4096], P(None, 'ctx'), may hold values from -0.75 to 0.75
- skip_gain: float32 [4096], P('ctx'), may hold values from -3 to 3
Outputs:
- grad_projected: bfloat16 [2, 8, 512, 4096], P(None, 'dp', 'ctx')
- grad_short: float32 [2, 7, 4096], P(None, None, 'ctx')
- grad_medium: float32 [128, 4096], P(None, 'ctx')
- grad_skip: float32 [4096], P('ctx')
All inputs are finite; a program needn't handle non-finite values.
Results may differ from a plain program's by a relative error of at most 0.024.
Values may be sent and summed in bfloat16 or wider, within the bound.
A program may use at most 128 MiB of HBM per device.

v0:
```python
import functools

import jax
import jax.numpy as jnp
import ml_dtypes
import numpy as np
from jax import lax
from jax.experimental import pallas as pl
from jax.experimental.pallas import tpu as pltpu
from jax.sharding import PartitionSpec as P

MESH = pl.DeviceIdType.MESH
F32 = jnp.float32
BF16 = jnp.bfloat16
LANES = 128
EDGE = 16


def transform_table(block):
    bins = np.concatenate([np.arange(0, block, 2), np.arange(1, block, 2)])
    angle = 2 * np.pi * np.outer(bins + 0.5, np.arange(block)) / (2 * block)
    return np.concatenate([np.cos(angle), -np.sin(angle)])


def quarter_turn(spec):
    half = spec.shape[0] // 4
    re_even, re_odd = spec[:half], spec[half : 2 * half]
    im_even, im_odd = spec[2 * half : 3 * half], spec[3 * half :]
    return jnp.concatenate([-im_even, im_odd, re_even, -re_odd], axis=0)


def times(a, b):
    half = a.shape[0] // 2
    ar, ai, br, bi = a[:half], a[half:], b[:half], b[half:]
    return jnp.concatenate([ar * br - ai * bi, ar * bi + ai * br], axis=0)


def times_conj(a, b):
    half = a.shape[0] // 2
    ar, ai, br, bi = a[:half], a[half:], b[:half], b[half:]
    return jnp.concatenate([ar * br + ai * bi, ai * br - ar * bi], axis=0)


def kernel(
    n,
    chunks,
    x_ref,
    tok_ref,
    short_ref,
    medium_ref,
    skip_ref,
    fwd_ref,
    inv_ref,
    out_ref,
    grads_ref,
    xin,
    xf,
    filt,
    sfull,
    wrow,
    wtile,
    prod_send,
    prod_recv,
    b_send,
    b_recv,
    out_v,
    gbuf,
    gs_f,
    gs_send,
    gs_recv,
    zs,
    gspec,
    gmix,
    halo_ssem,
    halo_rsem,
    small_ssem,
    small_rsem,
    p_ssem,
    p_rsem,
    b_ssem,
    b_rsem,
    g_ssem,
    g_rsem,
    in_sem,
    out_sem,
):
    me = lax.axis_index("ctx")
    dp = lax.axis_index("dp")
    block = x_ref.shape[1]
    own = medium_ref.shape[1]
    width = own // chunks
    tiles = width // LANES
    short_len = short_ref.shape[1]
    rows = block + EDGE
    order = [d for d in (2, 1, 3) if d < n] + [d for d in range(4, n)]

    def peer(d):
        return lax.rem(me + d, n)

    def remote(src, dst, ssem, rsem, to):
        return pltpu.make_async_remote_copy(
            src_ref=src,
            dst_ref=dst,
            send_sem=ssem,
            recv_sem=rsem,
            device_id=(dp, to),
            device_id_type=MESH,
        )

    local_in = pltpu.make_async_copy(x_ref, xin.at[:, pl.ds(EDGE, block), :], in_sem)
    local_in.start()
    tokens = tok_ref[...]
    weight = jnp.where((tokens >= 97) & (tokens <= 122), 0.1, 1.0).astype(BF16).astype(F32)
    wrow[me] = jnp.broadcast_to(weight, (8, block))
    sfull[me] = short_ref[...]

    barrier = pltpu.get_barrier_semaphore()
    for d in order:
        pl.semaphore_signal(barrier, inc=1, device_id=(dp, peer(d)), device_id_type=MESH)
    pl.semaphore_wait(barrier, n - 1)

    later = lax.rem(me + 1, n)
    earlier = lax.rem(me + n - 1, n)
    to_later = remote(
        x_ref.at[:, pl.ds(block - EDGE, EDGE), :],
        xin.at[:, pl.ds(0, EDGE), :],
        halo_ssem.at[0],
        halo_rsem.at[0],
        later,
    )
    to_earlier = remote(
        x_ref.at[:, pl.ds(0, EDGE), :],
        xin.at[:, pl.ds(block + EDGE, EDGE), :],
        halo_ssem.at[1],
        halo_rsem.at[1],
        earlier,
    )

    @pl.when(me < n - 1)
    def _():
        to_later.start()

    @pl.when(me > 0)
    def _():
        to_earlier.start()

    def small_copies(d, source):
        return (
            remote(
                sfull.at[source],
                sfull.at[source],
                small_ssem.at[0, d],
                small_rsem.at[0, source],
                peer(d),
            ),
            remote(
                wrow.at[source],
                wrow.at[source],
                small_ssem.at[1, d],
                small_rsem.at[1, source],
                peer(d),
            ),
        )

    for d in order:
        for copy in small_copies(d, me):
            copy.start()

    zero_edge = jnp.zeros((2, EDGE, xin.shape[2]), BF16)

    @pl.when(me == 0)
    def _():
        xin[:, pl.ds(0, EDGE), :] = zero_edge

    @pl.when(me == n - 1)
    def _():
        xin[:, pl.ds(block + EDGE, EDGE), :] = zero_edge

    b_send[pl.ds(n * block, EDGE), :] = jnp.zeros((EDGE, own), BF16)
    gs_f[...] = jnp.zeros_like(gs_f)

    for d in order:
        for copy in small_copies(d, peer(d)):
            copy.wait_recv()
    for o in range(n):
        wtile[pl.ds(o * block, block), :] = jnp.broadcast_to(wrow[o, 0:1, :], (LANES, block)).T
    local_in.wait()

    @pl.when(me > 0)
    def _():
        to_later.wait_recv()

    @pl.when(me < n - 1)
    def _():
        to_earlier.wait_recv()

    def columns(owner, k):
        return pl.ds(pl.multiple_of(owner * own + k * width, LANES), width)

    def prod_copy(k, d, source):
        return remote(
            prod_send.at[:, columns(peer(d), k)],
            prod_recv.at[pl.ds(pl.multiple_of(source * block, block), block), columns(0, k)],
            p_ssem.at[k, d],
            p_rsem.at[k, source],
            peer(d),
        )

    def back_copy(k, d, source):
        return remote(
            b_send.at[pl.ds(pl.multiple_of(peer(d) * block, block), rows), columns(0, k)],
            b_recv.at[:, columns(source, k)],
            b_ssem.at[k, d],
            b_rsem.at[k, source],
            peer(d),
        )

    def short_copy(k, d, source):
        return remote(
            gs_send.at[:, columns(peer(d), k)],
            gs_recv.at[source, :, columns(0, k)],
            g_ssem.at[k, d],
            g_rsem.at[k, source],
            peer(d),
        )

    def out_copy(k, owner):
        return pltpu.make_async_copy(
            out_v.at[:, :, columns(owner, k)],
            out_ref.at[:, :, columns(owner, k)],
            out_sem.at[k, owner],
        )

    def products(k):
        for d in order + [0]:
            owner = peer(d)

            @pl.loop(0, tiles)
            def _(tile):
                inner = pl.ds(pl.multiple_of(k * width + tile * LANES, LANES), LANES)
                cols = pl.ds(pl.multiple_of(owner * own + k * width + tile * LANES, LANES), LANES)
                for s in range(2):
                    xf[s, :, cols] = xin[s, :, cols].astype(F32)
                    total = jnp.zeros((rows, LANES), F32)
                    for i in range(short_len):
                        total += sfull[owner, s, i : i + 1, inner] * xf[s, pl.ds(EDGE - i, rows), cols]
                    filt[s, :, cols] = total
                product = (filt[0, pl.ds(0, block), cols] * filt[1, pl.ds(0, block), cols]).astype(BF16)
                if d == 0:
                    prod_recv[pl.ds(pl.multiple_of(me * block, block), block), inner] = product
                else:
                    prod_send[:, cols] = product

            if d != 0:
                prod_copy(k, d, me).start()

    def medium(k):
        for d in order:
            prod_copy(k, d, peer(d)).wait_recv()
        cols = columns(0, k)
        fwd = fwd_ref[...]
        inv = inv_ref[...]
        skip = skip_ref[:, cols]

        def block_rows(f):
            return pl.ds(f * block, block)

        def dot(a, b):
            return jnp.dot(a, b, preferred_element_type=F32)

        response = dot(fwd, medium_ref[:, cols])
        for f in range(n):
            gspec[f] = dot(fwd, prod_recv[block_rows(f), cols])
        for f in range(n):
            zs[f] = gspec[f] + quarter_turn(gspec[f - 1]) if f else gspec[f]
        gain = jnp.zeros((1, width), F32)
        for f in range(n):
            product = prod_recv[block_rows(f), cols].astype(F32)
            mix = dot(inv, times(response, zs[f]).astype(BF16)) + skip * product
            weights = jnp.concatenate([wtile[block_rows(f), :]] * tiles, axis=1)
            grad = (weights * mix).astype(BF16)
            gmix[block_rows(f), :] = grad
            gain += jnp.sum(grad.astype(F32) * product, axis=0, keepdims=True)
        for f in range(n):
            gspec[f] = dot(fwd, gmix[block_rows(f), :])
        cross = jnp.zeros((2 * block, width), F32)
        for f in range(n):
            cross += times_conj(gspec[f], zs[f])
        for f in range(n):
            spec = gspec[f] - quarter_turn(gspec[f + 1]) if f < n - 1 else gspec[f]
            back = dot(inv, times_conj(spec, response).astype(BF16))
            back += skip * gmix[block_rows(f), :].astype(F32)
            b_send[block_rows(f), cols] = back.astype(BF16)
        for d in order:
            back_copy(k, d, me).start()
        high = cross.astype(BF16)
        low = (cross - high.astype(F32)).astype(BF16)
        grads_ref[pl.ds(0, block), cols] = (dot(inv, high) + dot(inv, low)).astype(BF16)
        gs_f[2 * short_len : 2 * short_len + 1, columns(me, k)] = gain

    def shorts(k):
        for d in [0] + order:
            owner = peer(d)
            if d != 0:
                back_copy(k, d, owner).wait_recv()

            @pl.loop(0, tiles)
            def _(tile):
                inner = pl.ds(pl.multiple_of(k * width + tile * LANES, LANES), LANES)
                cols = pl.ds(pl.multiple_of(owner * own + k * width + tile * LANES, LANES), LANES)
                if d == 0:
                    back = b_send[pl.ds(pl.multiple_of(me * block, block), rows), inner].astype(F32)
                else:
                    back = b_recv[:, cols].astype(F32)
                for s in range(2):
                    gbuf[s] = (back * filt[1 - s, :, cols]).astype(BF16).astype(F32)
                    total = jnp.zeros((block, LANES), F32)
                    grad = gbuf[s, pl.ds(0, block), :]
                    for i in range(short_len):
                        total += sfull[owner, s, i : i + 1, inner] * gbuf[s, pl.ds(i, block), :]
                        row = s * short_len + i
                        gs_f[row : row + 1, cols] = jnp.sum(
                            grad * xf[s, pl.ds(EDGE - i, block), cols], axis=0, keepdims=True
                        )
                    out_v[s, :, cols] = total.astype(BF16)

            out_copy(k, owner).start()
            if d != 0:
                gs_send[:, columns(owner, k)] = gs_f[:, columns(owner, k)].astype(BF16)
                short_copy(k, d, me).start()

    @pl.loop(0, chunks + 2)
    def _(step):
        @pl.when(step < chunks)
        def _():
            products(step)

        @pl.when((step >= 1) & (step <= chunks))
        def _():
            medium(step - 1)

        @pl.when(step >= 2)
        def _():
            shorts(step - 2)

    @pl.loop(0, chunks)
    def _(k):
        total = gs_f[:, columns(me, k)]
        for d in order:
            short_copy(k, d, peer(d)).wait_recv()
            total += gs_recv[peer(d), :, columns(0, k)].astype(F32)
        grads_ref[pl.ds(block, EDGE), columns(0, k)] = total.astype(BF16)
        for d in order:
            prod_copy(k, d, me).wait_send()
            back_copy(k, d, me).wait_send()
            short_copy(k, d, me).wait_send()
        for o in range(n):
            out_copy(k, o).wait()

    for d in order:
        for copy in small_copies(d, me):
            copy.wait_send()

    @pl.when(me < n - 1)
    def _():
        to_later.wait_send()

    @pl.when(me > 0)
    def _():
        to_earlier.wait_send()


def local(projected, token_ids, short_filters, medium_filter, skip_gain):
    inputs = projected[:, 0]
    _, block, channels = inputs.shape
    short_len = short_filters.shape[1]
    own = medium_filter.shape[1]
    groups = lax.axis_size("dp")
    n = lax.axis_size("ctx")
    chunks = max(1, own // 256)
    width = own // chunks
    table = transform_table(block)
    forward = jnp.asarray(table.astype(ml_dtypes.bfloat16))
    inverse = jnp.asarray((table.T / block).astype(ml_dtypes.bfloat16))
    rows = block + EDGE
    vmem = pl.BlockSpec(memory_space=pltpu.VMEM)
    hbm = pl.BlockSpec(memory_space=pl.ANY)
    dma = pltpu.SemaphoreType.DMA
    out, grads = pl.pallas_call(
        functools.partial(kernel, n, chunks),
        out_shape=(
            jax.ShapeDtypeStruct(inputs.shape, BF16),
            jax.ShapeDtypeStruct((rows, own), BF16),
        ),
        in_specs=[hbm, vmem, vmem, vmem, vmem, vmem, vmem],
        out_specs=(hbm, vmem),
        scratch_shapes=[
            pltpu.VMEM((2, block + 2 * EDGE, channels), BF16),
            pltpu.VMEM((2, block + 2 * EDGE, channels), F32),
            pltpu.VMEM((2, rows, channels), F32),
            pltpu.VMEM((n, 2, short_len, own), F32),
            pltpu.VMEM((n, 8, block), F32),
            pltpu.VMEM((n * block, LANES), F32),
            pltpu.VMEM((block, channels), BF16),
            pltpu.VMEM((n * block, own), BF16),
            pltpu.VMEM((n * block + EDGE, own), BF16),
            pltpu.VMEM((rows, channels), BF16),
            pltpu.VMEM((2, block, channels), BF16),
            pltpu.VMEM((2, rows, LANES), F32),
            pltpu.VMEM((EDGE, channels), F32),
            pltpu.VMEM((EDGE, channels), BF16),
            pltpu.VMEM((n, EDGE, own), BF16),
            pltpu.VMEM((n, 2 * block, width), F32),
            pltpu.VMEM((n, 2 * block, width), F32),
            pltpu.VMEM((n * block, width), BF16),
            dma((2,)),
            dma((2,)),
            dma((2, n)),
            dma((2, n)),
            dma((chunks, n)),
            dma((chunks, n)),
            dma((chunks, n)),
            dma((chunks, n)),
            dma((chunks, n)),
            dma((chunks, n)),
            dma,
            dma((chunks, n)),
        ],
        compiler_params=pltpu.CompilerParams(
            collective_id=0, has_side_effects=True, vmem_limit_bytes=48 * 1024 * 1024
        ),
    )(inputs, token_ids, short_filters, medium_filter, skip_gain[None], forward, inverse)
    grads = lax.psum(grads, "dp").astype(F32) / groups
    taps = grads[:block]
    short = grads[block : block + 2 * short_len].reshape(2, short_len, own)
    gain = grads[block + 2 * short_len]
    return out[:, None], short, taps, gain


def solution(mesh):
    placed = (
        P(None, "dp", "ctx", None),
        P("dp", "ctx"),
        P(None, None, "ctx"),
        P(None, "ctx"),
        P("ctx"),
    )
    return jax.shard_map(
        local,
        mesh=mesh,
        in_specs=placed,
        out_specs=(P(None, "dp", "ctx", None), P(None, None, "ctx"), P(None, "ctx"), P("ctx")),
        check_vma=False,
    )
```

profile of v0, /device:TPU:0, one launch (start us, length us, event | category | flops | bytes accessed | tf_op | source)
XLA Modules:
  0.0 139.2 jit_solution(7026117887395954043)
XLA Ops:
  7.2 0.0 all-reduce.2.cloned.1.call-start
  7.2 0.8 copy.14.short_ref
  8.1 0.0 copy-start
  8.1 1.6 %copy-done = bf16[2,1,128,4096]{3,2,1,0:T(8,128)(2,1)S(1)} copy-done((bf16[2,1,128,4096]{3,2,1,0:T(8,128)(2,1)S(1)}, bf16[2,1,128,4096]{3,2,1,0:T(8,128)(2,1)}, u32[]{:S(2)}) %copy-start) | copy-done | bytes 2097176
  9.7 0.0 copy-start.1
  9.7 0.9 copy-done.1
  10.6 0.0 copy-start.2
  10.6 0.8 copy-done.2
  11.4 0.0 copy-start.3
  11.4 0.8 copy-done.3
  12.3 0.0 copy-start.4
  12.3 0.7 copy-done.4
  13.0 0.0 copy-start.5
  13.0 0.7 copy-done.5
  13.6 42.4 %shard_map.102 = (bf16[2,128,4096]{2,1,0:T(8,128)(2,1)S(1)}, bf16[144,1024]{1,0:T(8,128)(2,1)}) custom-call(bf16[2,128,4096]{2,1,0:T(8,128)(2,1)S(1)} %bitcast.6, s32[1,128]{1,0:T(1,128)S(1)} %copy-done.5, f32[2,7,1024]{2,1,0:T(8,128)S(1)} %copy.14.short_ref, bf16[128,1024]{1,0:T(8,128)(2,1)S(1)} %copy-done.1, f32[1,1024]{1,0:T(1,128)S(1)} %bitcast.8, ...), custom_call_target="tpu_custom_call" | custom-call | tf_op jit(solution)/shard_map/pallas_call | solution.py:389
  56.0 0.0 all-reduce.2.cloned.1.call-update
  56.0 71.9 %all-reduce.2.cloned.1.call-done = bf16[144,1024]{1,0:T(8,128)(2,1)} async-done(((bf16[144,1024]{1,0:T(8,128)(2,1)}), bf16[144,1024]{1,0:T(8,128)(2,1)}) %all-reduce.2.cloned.1.call-update) | async-done | bytes 294928 | tf_op jit(solution)/shard_map/psum | solution.py:433
  127.9 1.0 convert_multiply_fusion
  128.9 0.6 slice.14
  129.5 0.8 slice.13
  130.4 0.7 copy.16
  131.0 1.3 copy.19
  (2 shorter events, 0.0 us)
Async XLA Ops:
  7.2 120.7 %all-reduce.2.cloned.1.call-start = ((), (), s32[]{:S(2)}) async-start(), calls=%async_computation | async-start | bytes 589824 | tf_op jit(solution)/shard_map/psum | solution.py:433
  8.1 1.6 %copy-start = (bf16[2,1,128,4096]{3,2,1,0:T(8,128)(2,1)S(1)}, bf16[2,1,128,4096]{3,2,1,0:T(8,128)(2,1)}, u32[]{:S(2)}) copy-start(bf16[2,1,128,4096]{3,2,1,0:T(8,128)(2,1)} %param.7) | copy-start | bytes 6291460
  9.7 0.9 copy-start.1
  10.6 0.8 copy-start.2
  11.4 0.8 copy-start.3
  12.3 0.7 copy-start.4
  13.0 0.7 copy-start.5
Sparse Core Ops, SparseCore 0:
  56.1 71.7 all-reduce.1
where the time goes:
time: 140 us; the launch traced here: 139 us
  waiting for transfers between devices  71.9 us (51%)
  Pallas kernels  42.4 us (30%)
  between operations  14.1 us (10%)
  local copies, waits for them, and re-layouts  9.83 us (7%)
    psum x1, waiting for transfers between devices, local(): grads = lax.psum(grads, 'dp').astype(F32) / groups  71.9 us
    pallas_call x1, Pallas kernels, local(): pl.pallas_call(functools.partial(kernel, n, chunks), out_shape=(jax.Shape...  42.4 us
    unnamed x15, local copies, waits for them, and re-layouts  8.39 us
  transfers between devices with their start and end apart: 1, of which 1 were waited for; matrix products, arithmetic and copies ran while one was open for 0% of the time, Pallas kernels for 0%

commit v1 on v0

--- a/solution.py
+++ b/solution.py
@@ -43,16 +43,31 @@
 
 def kernel(
     n,
+    groups,
     chunks,
+    fused,
     x_ref,
+    tok_hbm,
+    short_hbm,
+    medium_hbm,
+    skip_hbm,
+    fwd_hbm,
+    inv_hbm,
+    out_ref,
+    taps_ref,
+    short_out,
+    gain_ref,
     tok_ref,
-    short_ref,
     medium_ref,
     skip_ref,
     fwd_ref,
     inv_ref,
-    out_ref,
-    grads_ref,
+    part,
+    part_recv,
+    piece,
+    gathered,
+    gs_sum,
+    gs_all,
     xin,
     xf,
     filt,
@@ -81,6 +96,12 @@
     b_rsem,
     g_ssem,
     g_rsem,
+    r_ssem,
+    r_rsem,
+    a_ssem,
+    a_rsem,
+    t_ssem,
+    t_rsem,
     in_sem,
     out_sem,
 ):
@@ -90,34 +111,55 @@
     own = medium_ref.shape[1]
     width = own // chunks
     tiles = width // LANES
-    short_len = short_ref.shape[1]
+    short_len = short_hbm.shape[0]
     rows = block + EDGE
     order = [d for d in (2, 1, 3) if d < n] + [d for d in range(4, n)]
 
     def peer(d):
         return lax.rem(me + d, n)
 
-    def remote(src, dst, ssem, rsem, to):
+    def mate(e):
+        return lax.rem(dp + e, groups)
+
+    mates = range(1, groups) if fused else ()
+
+    def remote(src, dst, ssem, rsem, to, group=None):
         return pltpu.make_async_remote_copy(
             src_ref=src,
             dst_ref=dst,
             send_sem=ssem,
             recv_sem=rsem,
-            device_id=(dp, to),
+            device_id=(dp if group is None else group, to),
             device_id_type=MESH,
         )
 
-    local_in = pltpu.make_async_copy(x_ref, xin.at[:, pl.ds(EDGE, block), :], in_sem)
-    local_in.start()
+    loads = [
+        pltpu.make_async_copy(src, dst, in_sem.at[j])
+        for j, (src, dst) in enumerate(
+            (
+                (tok_hbm, tok_ref),
+                (short_hbm, sfull.at[me]),
+                (x_ref, xin.at[:, pl.ds(EDGE, block), :]),
+                (medium_hbm, medium_ref),
+                (skip_hbm, skip_ref),
+                (fwd_hbm, fwd_ref),
+                (inv_hbm, inv_ref),
+            )
+        )
+    ]
+    for load in loads:
+        load.start()
+    loads[0].wait()
     tokens = tok_ref[...]
     weight = jnp.where((tokens >= 97) & (tokens <= 122), 0.1, 1.0).astype(BF16).astype(F32)
     wrow[me] = jnp.broadcast_to(weight, (8, block))
-    sfull[me] = short_ref[...]
 
     barrier = pltpu.get_barrier_semaphore()
     for d in order:
         pl.semaphore_signal(barrier, inc=1, device_id=(dp, peer(d)), device_id_type=MESH)
-    pl.semaphore_wait(barrier, n - 1)
+    for e in mates:
+        pl.semaphore_signal(barrier, inc=1, device_id=(mate(e), me), device_id_type=MESH)
+    pl.semaphore_wait(barrier, n - 1 + len(mates))
 
     later = lax.rem(me + 1, n)
     earlier = lax.rem(me + n - 1, n)
@@ -162,6 +204,7 @@
             ),
         )
 
+    loads[1].wait()
     for d in order:
         for copy in small_copies(d, me):
             copy.start()
@@ -184,7 +227,8 @@
             copy.wait_recv()
     for o in range(n):
         wtile[pl.ds(o * block, block), :] = jnp.broadcast_to(wrow[o, 0:1, :], (LANES, block)).T
-    local_in.wait()
+    for load in loads[2:]:
+        load.wait()
 
     @pl.when(me > 0)
     def _():
@@ -222,6 +266,36 @@
             g_ssem.at[k, d],
             g_rsem.at[k, source],
             peer(d),
+        )
+
+    def scatter_copy(k, e, source):
+        return remote(
+            part.at[pl.ds(pl.multiple_of(mate(e) * EDGE, EDGE), EDGE), columns(0, k)],
+            part_recv.at[source, :, columns(0, k)],
+            r_ssem.at[k, e],
+            r_rsem.at[k, source],
+            me,
+            mate(e),
+        )
+
+    def gather_copy(k, e, source):
+        return remote(
+            piece.at[:, columns(0, k)],
+            gathered.at[pl.ds(pl.multiple_of(source * EDGE, EDGE), EDGE), columns(0, k)],
+            a_ssem.at[k, e],
+            a_rsem.at[k, source],
+            me,
+            mate(e),
+        )
+
+    def share_copy(k, e, source):
+        return remote(
+            gs_sum.at[:, columns(0, k)],
+            gs_all.at[source, :, columns(0, k)],
+            t_ssem.at[k, e],
+            t_rsem.at[k, source],
+            me,
+            mate(e),
         )
 
     def out_copy(k, owner):
@@ -243,7 +317,7 @@
                     xf[s, :, cols] = xin[s, :, cols].astype(F32)
                     total = jnp.zeros((rows, LANES), F32)
                     for i in range(short_len):
-                        total += sfull[owner, s, i : i + 1, inner] * xf[s, pl.ds(EDGE - i, rows), cols]
+                        total += sfull[owner, i, s : s + 1, inner] * xf[s, pl.ds(EDGE - i, rows), cols]
                     filt[s, :, cols] = total
                 product = (filt[0, pl.ds(0, block), cols] * filt[1, pl.ds(0, block), cols]).astype(BF16)
                 if d == 0:
@@ -295,7 +369,13 @@
             back_copy(k, d, me).start()
         high = cross.astype(BF16)
         low = (cross - high.astype(F32)).astype(BF16)
-        grads_ref[pl.ds(0, block), cols] = (dot(inv, high) + dot(inv, low)).astype(BF16)
+        taps = dot(inv, high) + dot(inv, low)
+        if fused:
+            part[:, cols] = taps.astype(BF16)
+            for e in mates:
+                scatter_copy(k, e, dp).start()
+        else:
+            taps_ref[:, cols] = taps
         gs_f[2 * short_len : 2 * short_len + 1, columns(me, k)] = gain
 
     def shorts(k):
@@ -317,7 +397,7 @@
                     total = jnp.zeros((block, LANES), F32)
                     grad = gbuf[s, pl.ds(0, block), :]
                     for i in range(short_len):
-                        total += sfull[owner, s, i : i + 1, inner] * gbuf[s, pl.ds(i, block), :]
+                        total += sfull[owner, i, s : s + 1, inner] * gbuf[s, pl.ds(i, block), :]
                         row = s * short_len + i
                         gs_f[row : row + 1, cols] = jnp.sum(
                             grad * xf[s, pl.ds(EDGE - i, block), cols], axis=0, keepdims=True
@@ -329,6 +409,39 @@
                 gs_send[:, columns(owner, k)] = gs_f[:, columns(owner, k)].astype(BF16)
                 short_copy(k, d, me).start()
 
+    def reduce_taps(k):
+        cols = columns(0, k)
+        total = part[pl.ds(pl.multiple_of(dp * EDGE, EDGE), EDGE), cols].astype(F32)
+        for e in mates:
+            scatter_copy(k, e, mate(e)).wait_recv()
+        for e in mates:
+            total += part_recv[mate(e), :, cols].astype(F32)
+        piece[:, cols] = total.astype(BF16)
+        for e in mates:
+            gather_copy(k, e, dp).start()
+        gathered[pl.ds(pl.multiple_of(dp * EDGE, EDGE), EDGE), cols] = total.astype(BF16)
+
+    def reduce_shorts(k):
+        cols = columns(0, k)
+        total = gs_f[:, columns(me, k)]
+        for d in order:
+            short_copy(k, d, peer(d)).wait_recv()
+        for d in order:
+            total += gs_recv[peer(d), :, cols].astype(F32)
+        if fused:
+            gs_sum[:, cols] = total.astype(BF16)
+            for e in mates:
+                share_copy(k, e, dp).start()
+        else:
+            write_shorts(cols, total)
+
+    def write_shorts(cols, total):
+        for s in range(2):
+            for i in range(short_len):
+                row = s * short_len + i
+                short_out[i, s : s + 1, cols] = total[row : row + 1]
+        gain_ref[:, cols] = total[2 * short_len : 2 * short_len + 1]
+
     @pl.loop(0, chunks + 2)
     def _(step):
         @pl.when(step < chunks)
@@ -339,23 +452,49 @@
         def _():
             medium(step - 1)
 
+        if fused:
+
+            @pl.when(step >= 2)
+            def _():
+                reduce_taps(step - 2)
+
         @pl.when(step >= 2)
         def _():
             shorts(step - 2)
 
+        @pl.when(step >= 3)
+        def _():
+            reduce_shorts(step - 3)
+
+    reduce_shorts(chunks - 1)
+
     @pl.loop(0, chunks)
     def _(k):
-        total = gs_f[:, columns(me, k)]
-        for d in order:
-            short_copy(k, d, peer(d)).wait_recv()
-            total += gs_recv[peer(d), :, columns(0, k)].astype(F32)
-        grads_ref[pl.ds(block, EDGE), columns(0, k)] = total.astype(BF16)
         for d in order:
             prod_copy(k, d, me).wait_send()
             back_copy(k, d, me).wait_send()
             short_copy(k, d, me).wait_send()
         for o in range(n):
             out_copy(k, o).wait()
+        for e in mates:
+            scatter_copy(k, e, dp).wait_send()
+            gather_copy(k, e, dp).wait_send()
+            share_copy(k, e, dp).wait_send()
+
+    if fused:
+
+        @pl.loop(0, chunks)
+        def _(k):
+            cols = columns(0, k)
+            for e in mates:
+                gather_copy(k, e, mate(e)).wait_recv()
+            taps_ref[:, cols] = gathered[:, cols].astype(F32) / groups
+            total = gs_sum[:, cols].astype(F32)
+            for e in mates:
+                share_copy(k, e, mate(e)).wait_recv()
+            for e in mates:
+                total += gs_all[mate(e), :, cols].astype(F32)
+            write_shorts(cols, total / groups)
 
     for d in order:
         for copy in small_copies(d, me):
@@ -386,19 +525,34 @@
     vmem = pl.BlockSpec(memory_space=pltpu.VMEM)
     hbm = pl.BlockSpec(memory_space=pl.ANY)
     dma = pltpu.SemaphoreType.DMA
-    out, grads = pl.pallas_call(
-        functools.partial(kernel, n, chunks),
+    fused = block == EDGE * groups
+    held = groups if fused else 1
+    out, taps, short, gain = pl.pallas_call(
+        functools.partial(kernel, n, groups, chunks, fused),
         out_shape=(
             jax.ShapeDtypeStruct(inputs.shape, BF16),
-            jax.ShapeDtypeStruct((rows, own), BF16),
+            jax.ShapeDtypeStruct((block, own), F32),
+            jax.ShapeDtypeStruct((short_len, 2, own), F32),
+            jax.ShapeDtypeStruct((1, own), F32),
         ),
-        in_specs=[hbm, vmem, vmem, vmem, vmem, vmem, vmem],
-        out_specs=(hbm, vmem),
+        in_specs=[hbm] * 7,
+        out_specs=(hbm, vmem, vmem, vmem),
         scratch_shapes=[
+            pltpu.VMEM((1, block), jnp.int32),
+            pltpu.VMEM((block, own), BF16),
+            pltpu.VMEM((1, own), F32),
+            pltpu.VMEM((2 * block, block), BF16),
+            pltpu.VMEM((block, 2 * block), BF16),
+            pltpu.VMEM((block, own), BF16),
+            pltpu.VMEM((held, EDGE, own), BF16),
+            pltpu.VMEM((EDGE, own), BF16),
+            pltpu.VMEM((block, own), BF16),
+            pltpu.VMEM((EDGE, own), BF16),
+            pltpu.VMEM((held, EDGE, own), BF16),
             pltpu.VMEM((2, block + 2 * EDGE, channels), BF16),
             pltpu.VMEM((2, block + 2 * EDGE, channels), F32),
             pltpu.VMEM((2, rows, channels), F32),
-            pltpu.VMEM((n, 2, short_len, own), F32),
+            pltpu.VMEM((n, short_len, 2, own), F32),
             pltpu.VMEM((n, 8, block), F32),
             pltpu.VMEM((n * block, LANES), F32),
             pltpu.VMEM((block, channels), BF16),
@@ -423,18 +577,24 @@
             dma((chunks, n)),
             dma((chunks, n)),
             dma((chunks, n)),
-            dma,
+            dma((chunks, held)),
+            dma((chunks, held)),
+            dma((chunks, held)),
+            dma((chunks, held)),
+            dma((chunks, held)),
+            dma((chunks, held)),
+            dma((7,)),
             dma((chunks, n)),
         ],
         compiler_params=pltpu.CompilerParams(
-            collective_id=0, has_side_effects=True, vmem_limit_bytes=48 * 1024 * 1024
+            collective_id=0, has_side_effects=True, vmem_limit_bytes=60 * 1024 * 1024
         ),
-    )(inputs, token_ids, short_filters, medium_filter, skip_gain[None], forward, inverse)
-    grads = lax.psum(grads, "dp").astype(F32) / groups
-    taps = grads[:block]
-    short = grads[block : block + 2 * short_len].reshape(2, short_len, own)
-    gain = grads[block + 2 * short_len]
-    return out[:, None], short, taps, gain
+    )(inputs, token_ids, short_filters.transpose(1, 0, 2), medium_filter, skip_gain[None], forward, inverse)
+    if not fused:
+        taps, short, gain = (
+            lax.psum(part.astype(BF16), "dp").astype(F32) / groups for part in (taps, short, gain)
+        )
+    return out[:, None], short.transpose(1, 0, 2), taps, gain[0]
 
 
 def solution(mesh):

time: 140 us -> 58 us (0.41)
  waiting for transfers between devices: 71.9 us -> 0 us
  between operations: 14.1 us -> 0.67 us
  Pallas kernels: 42.4 us -> 51.9 us
  local copies, waits for them, and re-layouts: 9.83 us -> 5.21 us
    psum x1 -> x0, waiting for transfers between devices: 71.9 us -> none  [local(): grads = lax.psum(grads, 'dp').astype(F32) / groups]
    pallas_call x1, Pallas kernels: 42.4 us -> 51.9 us  [local(): pl.pallas_call(functools.partial(kernel, n, groups, chunks, fused), out_s...]
    unnamed x15 -> x10, local copies, waits for them, and re-layouts: 8.39 us -> 5.21 us
    slice x3 -> x0, local copies, waits for them, and re-layouts: 1.44 us -> none  [the longest x1 0.83 us: local(): taps = grads[:block]]
  transfers between devices with their start and end apart: 1 -> 0, of which waited for: 1 -> 0; matrix products, arithmetic and copies ran while one was open for 0% -> 0% of each run, Pallas kernels for 0% -> 0%
where the time goes in v1:
time: 58 us; the launch traced here: 57.8 us
  Pallas kernels  51.9 us (89%)
  local copies, waits for them, and re-layouts  5.21 us (9%)
  between operations  0.67 us (1%)
    pallas_call x1, Pallas kernels, local(): pl.pallas_call(functools.partial(kernel, n, groups, chunks, fused), out_s...  51.9 us
    unnamed x10, local copies, waits for them, and re-layouts  5.21 us

profile of v1, /device:TPU:0, one launch (start us, length us, event | category | flops | bytes accessed | tf_op | source)
XLA Modules:
  0.0 57.8 jit_solution(17547231101586538273)
XLA Ops:
  0.6 51.9 %shard_map.102 = (bf16[2,128,4096]{2,1,0:T(8,128)(2,1)}, f32[128,1024]{1,0:T(8,128)}, f32[7,2,1024]{2,1,0:T(2,128)}, f32[1,1024]{1,0:T(1,128)}) custom-call(bf16[2,128,4096]{2,1,0:T(8,128)(2,1)} %bitcast.8, s32[1,128]{1,0:T(1,128)} %tok_hbm.1, f32[7,2,1024]{2,1,0:T(2,128)} %bitcast.11, bf16[128,1024]{1,0:T(8,128)(2,1)} %medium_hbm.1, f32[1,1024]{1,0:T(1,128)} %bitcast.12, ...), custom_call_target="tpu_custom_call" | custom-call | tf_op jit(solution)/shard_map/pallas_call | solution.py:530
  52.6 0.0 copy-start.1
  52.6 0.0 copy-start
  52.6 0.0 copy-start.2
  52.6 3.2 %copy.16 = bf16[2,1,128,4096]{3,2,1,0:T(8,128)(2,1)} copy(bf16[2,1,128,4096]{3,2,1,0:T(8,128)(2,1)} %bitcast.9) | data formatting | bytes 4194304
  55.8 0.0 copy-done.1
  55.8 0.6 %copy.17 = f32[2,7,1024]{2,0,1:T(2,128)} copy(f32[2,7,1024]{2,0,1:T(2,128)S(1)} %bitcast.10) | data formatting | bytes 114688
  56.4 0.0 copy-done
  56.4 0.8 %copy.18 = f32[128,1024]{1,0:T(8,128)} copy(f32[128,1024]{1,0:T(8,128)S(1)} %copy-done) | data formatting | bytes 1048576
  57.2 0.0 copy-done.2
  57.2 0.6 %copy.19 = f32[1024]{0:T(1024)} copy(f32[1024]{0:T(1024)S(1)} %bitcast.13) | data formatting | bytes 8192
Async XLA Ops:
  52.6 3.2 %copy-start.1 = (f32[7,2,1024]{2,1,0:T(2,128)S(1)}, f32[7,2,1024]{2,1,0:T(2,128)}, u32[]{:S(2)}) copy-start(f32[7,2,1024]{2,1,0:T(2,128)} %get-tuple-element.9) | copy-start | bytes 172036
  52.6 3.8 %copy-start = (f32[128,1024]{1,0:T(8,128)S(1)}, f32[128,1024]{1,0:T(8,128)}, u32[]{:S(2)}) copy-start(f32[128,1024]{1,0:T(8,128)} %get-tuple-element.22) | copy-start | bytes 1572868
  52.6 4.6 %copy-start.2 = (f32[1,1024]{1,0:T(1,128)S(1)}, f32[1,1024]{1,0:T(1,128)}, u32[]{:S(2)}) copy-start(f32[1,1024]{1,0:T(1,128)} %get-tuple-element.11) | copy-start | bytes 12292

commit v2 on v1

--- a/solution.py
+++ b/solution.py
@@ -86,8 +86,12 @@
     zs,
     gspec,
     gmix,
+    edge_ssem,
+    edge_rsem,
     halo_ssem,
     halo_rsem,
+    weight_ssem,
+    weight_rsem,
     small_ssem,
     small_rsem,
     p_ssem,
@@ -163,52 +167,64 @@
 
     later = lax.rem(me + 1, n)
     earlier = lax.rem(me + n - 1, n)
-    to_later = remote(
-        x_ref.at[:, pl.ds(block - EDGE, EDGE), :],
-        xin.at[:, pl.ds(0, EDGE), :],
-        halo_ssem.at[0],
-        halo_rsem.at[0],
-        later,
-    )
+
+    def columns(owner, k):
+        return pl.ds(pl.multiple_of(owner * own + k * width, LANES), width)
+
+    def edge_copy(k, owner):
+        return remote(
+            x_ref.at[:, pl.ds(block - EDGE, EDGE), columns(owner, k)],
+            xin.at[:, pl.ds(0, EDGE), columns(owner, k)],
+            edge_ssem.at[k, owner],
+            edge_rsem.at[k, owner],
+            later,
+        )
+
     to_earlier = remote(
         x_ref.at[:, pl.ds(0, EDGE), :],
         xin.at[:, pl.ds(block + EDGE, EDGE), :],
-        halo_ssem.at[1],
-        halo_rsem.at[1],
+        halo_ssem,
+        halo_rsem,
         earlier,
     )
 
-    @pl.when(me < n - 1)
-    def _():
-        to_later.start()
+    def filter_copy(k, d, source):
+        return remote(
+            sfull.at[source, :, :, columns(0, k)],
+            sfull.at[source, :, :, columns(0, k)],
+            small_ssem.at[k, d],
+            small_rsem.at[k, source],
+            peer(d),
+        )
+
+    def weight_copy(d, source):
+        return remote(
+            wrow.at[source],
+            wrow.at[source],
+            weight_ssem.at[d],
+            weight_rsem.at[source],
+            peer(d),
+        )
+
+    loads[1].wait()
+
+    @pl.loop(0, chunks)
+    def _(k):
+        for d in order:
+            filter_copy(k, d, me).start()
+
+        @pl.when(me < n - 1)
+        def _():
+            for owner in range(n):
+                edge_copy(k, owner).start()
+
+    for d in order:
+        weight_copy(d, me).start()
 
     @pl.when(me > 0)
     def _():
         to_earlier.start()
 
-    def small_copies(d, source):
-        return (
-            remote(
-                sfull.at[source],
-                sfull.at[source],
-                small_ssem.at[0, d],
-                small_rsem.at[0, source],
-                peer(d),
-            ),
-            remote(
-                wrow.at[source],
-                wrow.at[source],
-                small_ssem.at[1, d],
-                small_rsem.at[1, source],
-                peer(d),
-            ),
-        )
-
-    loads[1].wait()
-    for d in order:
-        for copy in small_copies(d, me):
-            copy.start()
-
     zero_edge = jnp.zeros((2, EDGE, xin.shape[2]), BF16)
 
     @pl.when(me == 0)
@@ -222,24 +238,18 @@
     b_send[pl.ds(n * block, EDGE), :] = jnp.zeros((EDGE, own), BF16)
     gs_f[...] = jnp.zeros_like(gs_f)
 
-    for d in order:
-        for copy in small_copies(d, peer(d)):
-            copy.wait_recv()
-    for o in range(n):
-        wtile[pl.ds(o * block, block), :] = jnp.broadcast_to(wrow[o, 0:1, :], (LANES, block)).T
     for load in loads[2:]:
         load.wait()
 
-    @pl.when(me > 0)
-    def _():
-        to_later.wait_recv()
-
-    @pl.when(me < n - 1)
-    def _():
-        to_earlier.wait_recv()
-
-    def columns(owner, k):
-        return pl.ds(pl.multiple_of(owner * own + k * width, LANES), width)
+    def late_inputs():
+        for d in order:
+            weight_copy(d, peer(d)).wait_recv()
+        for o in range(n):
+            wtile[pl.ds(o * block, block), :] = jnp.broadcast_to(wrow[o, 0:1, :], (LANES, block)).T
+
+        @pl.when(me < n - 1)
+        def _():
+            to_earlier.wait_recv()
 
     def prod_copy(k, d, source):
         return remote(
@@ -306,6 +316,14 @@
         )
 
     def products(k):
+        for d in order:
+            filter_copy(k, d, peer(d)).wait_recv()
+
+        @pl.when(me > 0)
+        def _():
+            for owner in range(n):
+                edge_copy(k, owner).wait_recv()
+
         for d in order + [0]:
             owner = peer(d)
 
@@ -314,11 +332,11 @@
                 inner = pl.ds(pl.multiple_of(k * width + tile * LANES, LANES), LANES)
                 cols = pl.ds(pl.multiple_of(owner * own + k * width + tile * LANES, LANES), LANES)
                 for s in range(2):
-                    xf[s, :, cols] = xin[s, :, cols].astype(F32)
-                    total = jnp.zeros((rows, LANES), F32)
+                    xf[s, pl.ds(0, rows), cols] = xin[s, pl.ds(0, rows), cols].astype(F32)
+                    total = jnp.zeros((block, LANES), F32)
                     for i in range(short_len):
-                        total += sfull[owner, i, s : s + 1, inner] * xf[s, pl.ds(EDGE - i, rows), cols]
-                    filt[s, :, cols] = total
+                        total += sfull[owner, i, s : s + 1, inner] * xf[s, pl.ds(EDGE - i, block), cols]
+                    filt[s, pl.ds(0, block), cols] = total
                 product = (filt[0, pl.ds(0, block), cols] * filt[1, pl.ds(0, block), cols]).astype(BF16)
                 if d == 0:
                     prod_recv[pl.ds(pl.multiple_of(me * block, block), block), inner] = product
@@ -393,6 +411,12 @@
                 else:
                     back = b_recv[:, cols].astype(F32)
                 for s in range(2):
+                    xf[s, pl.ds(rows, EDGE), cols] = xin[s, pl.ds(rows, EDGE), cols].astype(F32)
+                    total = jnp.zeros((EDGE, LANES), F32)
+                    for i in range(short_len):
+                        total += sfull[owner, i, s : s + 1, inner] * xf[s, pl.ds(rows - i, EDGE), cols]
+                    filt[s, pl.ds(block, EDGE), cols] = total
+                for s in range(2):
                     gbuf[s] = (back * filt[1 - s, :, cols]).astype(BF16).astype(F32)
                     total = jnp.zeros((block, LANES), F32)
                     grad = gbuf[s, pl.ds(0, block), :]
@@ -442,29 +466,36 @@
                 short_out[i, s : s + 1, cols] = total[row : row + 1]
         gain_ref[:, cols] = total[2 * short_len : 2 * short_len + 1]
 
-    @pl.loop(0, chunks + 2)
+    ahead = min(2, chunks)
+    back_lag = ahead + min(2, chunks)
+
+    @pl.loop(0, chunks + back_lag)
     def _(step):
         @pl.when(step < chunks)
         def _():
             products(step)
 
-        @pl.when((step >= 1) & (step <= chunks))
-        def _():
-            medium(step - 1)
+        @pl.when(step == ahead)
+        def _():
+            late_inputs()
+
+        @pl.when((step >= ahead) & (step < chunks + ahead))
+        def _():
+            medium(step - ahead)
 
         if fused:
 
-            @pl.when(step >= 2)
+            @pl.when(step >= back_lag)
             def _():
-                reduce_taps(step - 2)
-
-        @pl.when(step >= 2)
-        def _():
-            shorts(step - 2)
-
-        @pl.when(step >= 3)
-        def _():
-            reduce_shorts(step - 3)
+                reduce_taps(step - back_lag)
+
+        @pl.when(step >= back_lag)
+        def _():
+            shorts(step - back_lag)
+
+        @pl.when(step >= back_lag + 1)
+        def _():
+            reduce_shorts(step - back_lag - 1)
 
     reduce_shorts(chunks - 1)
 
@@ -474,8 +505,15 @@
             prod_copy(k, d, me).wait_send()
             back_copy(k, d, me).wait_send()
             short_copy(k, d, me).wait_send()
+            filter_copy(k, d, me).wait_send()
         for o in range(n):
             out_copy(k, o).wait()
+
+        @pl.when(me < n - 1)
+        def _():
+            for owner in range(n):
+                edge_copy(k, owner).wait_send()
+
         for e in mates:
             scatter_copy(k, e, dp).wait_send()
             gather_copy(k, e, dp).wait_send()
@@ -497,12 +535,7 @@
             write_shorts(cols, total / groups)
 
     for d in order:
-        for copy in small_copies(d, me):
-            copy.wait_send()
-
-    @pl.when(me < n - 1)
-    def _():
-        to_later.wait_send()
+        weight_copy(d, me).wait_send()
 
     @pl.when(me > 0)
     def _():
@@ -567,10 +600,14 @@
             pltpu.VMEM((n, 2 * block, width), F32),
             pltpu.VMEM((n, 2 * block, width), F32),
             pltpu.VMEM((n * block, width), BF16),
-            dma((2,)),
-            dma((2,)),
-            dma((2, n)),
-            dma((2, n)),
+            dma((chunks, n)),
+            dma((chunks, n)),
+            dma,
+            dma,
+            dma((n,)),
+            dma((n,)),
+            dma((chunks, n)),
+            dma((chunks, n)),
             dma((chunks, n)),
             dma((chunks, n)),
             dma((chunks, n)),

time: 58 us -> 56.7 us (0.978)
  Pallas kernels: 51.9 us -> 50.7 us
    pallas_call x1, Pallas kernels: 51.9 us -> 50.7 us  [local(): pl.pallas_call(functools.partial(kernel, n, groups, chunks, fused), out_s...]
where the time goes in v2:
time: 56.7 us; the launch traced here: 56.6 us
  Pallas kernels  50.7 us (89%)
  local copies, waits for them, and re-layouts  5.21 us (9%)
  between operations  0.67 us (1%)
    pallas_call x1, Pallas kernels, local(): pl.pallas_call(functools.partial(kernel, n, groups, chunks, fused), out_s...  50.7 us
    unnamed x10, local copies, waits for them, and re-layouts  5.21 us

profile of v2, /device:TPU:0, one launch (start us, length us, event | category | flops | bytes accessed | tf_op | source)
XLA Modules:
  0.0 56.6 jit_solution(7096095443254099467)
XLA Ops:
  0.6 50.7 %shard_map.102 = (bf16[2,128,4096]{2,1,0:T(8,128)(2,1)}, f32[128,1024]{1,0:T(8,128)}, f32[7,2,1024]{2,1,0:T(2,128)}, f32[1,1024]{1,0:T(1,128)}) custom-call(bf16[2,128,4096]{2,1,0:T(8,128)(2,1)} %bitcast.8, s32[1,128]{1,0:T(1,128)} %tok_hbm.1, f32[7,2,1024]{2,1,0:T(2,128)} %bitcast.11, bf16[128,1024]{1,0:T(8,128)(2,1)} %medium_hbm.1, f32[1,1024]{1,0:T(1,128)} %bitcast.12, ...), custom_call_target="tpu_custom_call" | custom-call | tf_op jit(solution)/shard_map/pallas_call | solution.py:563
  51.3 0.0 copy-start.1
  51.3 0.0 copy-start
  51.3 0.0 copy-start.2
  51.4 3.2 %copy.16 = bf16[2,1,128,4096]{3,2,1,0:T(8,128)(2,1)} copy(bf16[2,1,128,4096]{3,2,1,0:T(8,128)(2,1)} %bitcast.9) | data formatting | bytes 4194304
  54.5 0.0 copy-done.1
  54.5 0.6 %copy.17 = f32[2,7,1024]{2,0,1:T(2,128)} copy(f32[2,7,1024]{2,0,1:T(2,128)S(1)} %bitcast.10) | data formatting | bytes 114688
  55.2 0.0 copy-done
  55.2 0.8 %copy.18 = f32[128,1024]{1,0:T(8,128)} copy(f32[128,1024]{1,0:T(8,128)S(1)} %copy-done) | data formatting | bytes 1048576
  56.0 0.0 copy-done.2
  56.0 0.6 %copy.19 = f32[1024]{0:T(1024)} copy(f32[1024]{0:T(1024)S(1)} %bitcast.13) | data formatting | bytes 8192
Async XLA Ops:
  51.3 3.2 %copy-start.1 = (f32[7,2,1024]{2,1,0:T(2,128)S(1)}, f32[7,2,1024]{2,1,0:T(2,128)}, u32[]{:S(2)}) copy-start(f32[7,2,1024]{2,1,0:T(2,128)} %get-tuple-element.9) | copy-start | bytes 172036
  51.3 3.8 %copy-start = (f32[128,1024]{1,0:T(8,128)S(1)}, f32[128,1024]{1,0:T(8,128)}, u32[]{:S(2)}) copy-start(f32[128,1024]{1,0:T(8,128)} %get-tuple-element.22) | copy-start | bytes 1572868
  51.3 4.6 %copy-start.2 = (f32[1,1024]{1,0:T(1,128)S(1)}, f32[1,1024]{1,0:T(1,128)}, u32[]{:S(2)}) copy-start(f32[1,1024]{1,0:T(1,128)} %get-tuple-element.11) | copy-start | bytes 12292

commit v3 on v2

--- a/solution.py
+++ b/solution.py
@@ -549,7 +549,7 @@
     own = medium_filter.shape[1]
     groups = lax.axis_size("dp")
     n = lax.axis_size("ctx")
-    chunks = max(1, own // 256)
+    chunks = max(1, own // 512)
     width = own // chunks
     table = transform_table(block)
     forward = jnp.asarray(table.astype(ml_dtypes.bfloat16))

time: 56.7 us -> 54.2 us (0.956)
  Pallas kernels: 50.7 us -> 48 us
    pallas_call x1, Pallas kernels: 50.7 us -> 48 us  [local(): pl.pallas_call(functools.partial(kernel, n, groups, chunks, fused), out_s...]
where the time goes in v3:
time: 54.2 us; the launch traced here: 53.9 us
  Pallas kernels  48 us (89%)
  local copies, waits for them, and re-layouts  5.21 us (10%)
  between operations  0.67 us (1%)
    pallas_call x1, Pallas kernels, local(): pl.pallas_call(functools.partial(kernel, n, groups, chunks, fused), out_s...  48 us
    unnamed x10, local copies, waits for them, and re-layouts  5.21 us

profile of v3, /device:TPU:0, one launch (start us, length us, event | category | flops | bytes accessed | tf_op | source)
XLA Modules:
  0.0 53.9 jit_solution(13515858003135820608)
XLA Ops:
  0.6 48.0 %shard_map.102 = (bf16[2,128,4096]{2,1,0:T(8,128)(2,1)}, f32[128,1024]{1,0:T(8,128)}, f32[7,2,1024]{2,1,0:T(2,128)}, f32[1,1024]{1,0:T(1,128)}) custom-call(bf16[2,128,4096]{2,1,0:T(8,128)(2,1)} %bitcast.8, s32[1,128]{1,0:T(1,128)} %tok_hbm.1, f32[7,2,1024]{2,1,0:T(2,128)} %bitcast.11, bf16[128,1024]{1,0:T(8,128)(2,1)} %medium_hbm.1, f32[1,1024]{1,0:T(1,128)} %bitcast.12, ...), custom_call_target="tpu_custom_call" | custom-call | tf_op jit(solution)/shard_map/pallas_call | solution.py:563
  48.7 0.0 copy-start.1
  48.7 0.0 copy-start
  48.7 0.0 copy-start.2
  48.7 3.2 %copy.16 = bf16[2,1,128,4096]{3,2,1,0:T(8,128)(2,1)} copy(bf16[2,1,128,4096]{3,2,1,0:T(8,128)(2,1)} %bitcast.9) | data formatting | bytes 4194304
  51.9 0.0 copy-done.1
  51.9 0.6 %copy.17 = f32[2,7,1024]{2,0,1:T(2,128)} copy(f32[2,7,1024]{2,0,1:T(2,128)S(1)} %bitcast.10) | data formatting | bytes 114688
  52.5 0.0 copy-done
  52.5 0.8 %copy.18 = f32[128,1024]{1,0:T(8,128)} copy(f32[128,1024]{1,0:T(8,128)S(1)} %copy-done) | data formatting | bytes 1048576
  53.3 0.0 copy-done.2
  53.3 0.6 %copy.19 = f32[1024]{0:T(1024)} copy(f32[1024]{0:T(1024)S(1)} %bitcast.13) | data formatting | bytes 8192
Async XLA Ops:
  48.7 3.2 %copy-start.1 = (f32[7,2,1024]{2,1,0:T(2,128)S(1)}, f32[7,2,1024]{2,1,0:T(2,128)}, u32[]{:S(2)}) copy-start(f32[7,2,1024]{2,1,0:T(2,128)} %get-tuple-element.9) | copy-start | bytes 172036
  48.7 3.8 %copy-start = (f32[128,1024]{1,0:T(8,128)S(1)}, f32[128,1024]{1,0:T(8,128)}, u32[]{:S(2)}) copy-start(f32[128,1024]{1,0:T(8,128)} %get-tuple-element.22) | copy-start | bytes 1572868
  48.7 4.6 %copy-start.2 = (f32[1,1024]{1,0:T(1,128)S(1)}, f32[1,1024]{1,0:T(1,128)}, u32[]{:S(2)}) copy-start(f32[1,1024]{1,0:T(1,128)} %get-tuple-element.11) | copy-start | bytes 12292

commit v4 on v3

--- a/solution.py
+++ b/solution.py
@@ -489,13 +489,13 @@
             def _():
                 reduce_taps(step - back_lag)
 
+        @pl.when(step >= back_lag + 1)
+        def _():
+            reduce_shorts(step - back_lag - 1)
+
         @pl.when(step >= back_lag)
         def _():
             shorts(step - back_lag)
-
-        @pl.when(step >= back_lag + 1)
-        def _():
-            reduce_shorts(step - back_lag - 1)
 
     reduce_shorts(chunks - 1)
 

time: 54.2 us -> 56.4 us (1.041)
  Pallas kernels: 48 us -> 50 us
    pallas_call x1, Pallas kernels: 48 us -> 50 us  [local(): pl.pallas_call(functools.partial(kernel, n, groups, chunks, fused), out_s...]
where the time goes in v4:
time: 56.4 us; the launch traced here: 55.8 us
  Pallas kernels  50 us (89%)
  local copies, waits for them, and re-layouts  5.21 us (9%)
  between operations  0.67 us (1%)
    pallas_call x1, Pallas kernels, local(): pl.pallas_call(functools.partial(kernel, n, groups, chunks, fused), out_s...  50 us
    unnamed x10, local copies, waits for them, and re-layouts  5.21 us

profile of v4, /device:TPU:0, one launch (start us, length us, event | category | flops | bytes accessed | tf_op | source)
XLA Modules:
  0.0 55.8 jit_solution(16792337781480961588)
XLA Ops:
  0.6 50.0 %shard_map.102 = (bf16[2,128,4096]{2,1,0:T(8,128)(2,1)}, f32[128,1024]{1,0:T(8,128)}, f32[7,2,1024]{2,1,0:T(2,128)}, f32[1,1024]{1,0:T(1,128)}) custom-call(bf16[2,128,4096]{2,1,0:T(8,128)(2,1)} %bitcast.8, s32[1,128]{1,0:T(1,128)} %tok_hbm.1, f32[7,2,1024]{2,1,0:T(2,128)} %bitcast.11, bf16[128,1024]{1,0:T(8,128)(2,1)} %medium_hbm.1, f32[1,1024]{1,0:T(1,128)} %bitcast.12, ...), custom_call_target="tpu_custom_call" | custom-call | tf_op jit(solution)/shard_map/pallas_call | solution.py:563
  50.6 0.0 copy-start.1
  50.6 0.0 copy-start
  50.6 0.0 copy-start.2
  50.6 3.2 %copy.16 = bf16[2,1,128,4096]{3,2,1,0:T(8,128)(2,1)} copy(bf16[2,1,128,4096]{3,2,1,0:T(8,128)(2,1)} %bitcast.9) | data formatting | bytes 4194304
  53.8 0.0 copy-done.1
  53.8 0.6 %copy.17 = f32[2,7,1024]{2,0,1:T(2,128)} copy(f32[2,7,1024]{2,0,1:T(2,128)S(1)} %bitcast.10) | data formatting | bytes 114688
  54.4 0.0 copy-done
  54.4 0.8 %copy.18 = f32[128,1024]{1,0:T(8,128)} copy(f32[128,1024]{1,0:T(8,128)S(1)} %copy-done) | data formatting | bytes 1048576
  55.2 0.0 copy-done.2
  55.2 0.6 %copy.19 = f32[1024]{0:T(1024)} copy(f32[1024]{0:T(1024)S(1)} %bitcast.13) | data formatting | bytes 8192
Async XLA Ops:
  50.6 3.2 %copy-start.1 = (f32[7,2,1024]{2,1,0:T(2,128)S(1)}, f32[7,2,1024]{2,1,0:T(2,128)}, u32[]{:S(2)}) copy-start(f32[7,2,1024]{2,1,0:T(2,128)} %get-tuple-element.9) | copy-start | bytes 172036
  50.6 3.8 %copy-start = (f32[128,1024]{1,0:T(8,128)S(1)}, f32[128,1024]{1,0:T(8,128)}, u32[]{:S(2)}) copy-start(f32[128,1024]{1,0:T(8,128)} %get-tuple-element.22) | copy-start | bytes 1572868
  50.6 4.6 %copy-start.2 = (f32[1,1024]{1,0:T(1,128)S(1)}, f32[1,1024]{1,0:T(1,128)}, u32[]{:S(2)}) copy-start(f32[1,1024]{1,0:T(1,128)} %get-tuple-element.11) | copy-start | bytes 12292
